TPU v7x, 256 devices: a whole 4x4x8 slice. The times are simulated.
256 devices in a mesh: row: 8 (over z_hi, core), col: 32 (over y, x, z_lo).
Axes of the slice: x: 4, y: 4, z: 8 (z_hi: 4, z_lo: 2; z = z_hi * 2 + z_lo), core: 2. Of those that a mesh axis runs over, the one named last changes fastest.
Arguments:
- matrix: bfloat16 [6144, 6144], P('col', 'row'), as said below
- pattern: int32 [48, 48], replicated, may hold values 0 or 1
- shift: float32 [6144], replicated, may hold values from 0.25 to 1
Outputs:
- square: bfloat16 [6144, 6144], P('col', 'row')
- updated: bfloat16 [6144, 6144], P('col', 'row')
Inputs may be any that keep to these rules, and one draw needn't show every extreme that they name: matrix is symmetric: the entry in row i and column j equals the entry in row j and column i.
All inputs are finite; a program needn't handle non-finite values.
Results may differ from a plain program's by a relative error of at most 0.0052.
Values may be sent and summed in bfloat16 or wider, within the bound.
A program may use at most 64 MiB of HBM per device.

v0:
```python
import jax
import jax.numpy as jnp
from jax import lax
from jax.sharding import PartitionSpec as P

BLOCK = 128
ORDER = 6144


def body(matrix, pattern, shift):
    rows_here, cols_here = matrix.shape
    count = pattern.shape[0]
    row_start = lax.axis_index("col") * rows_here
    col_start = lax.axis_index("row") * cols_here
    row_ids = row_start + jnp.arange(rows_here, dtype=jnp.int32)
    col_ids = col_start + jnp.arange(cols_here, dtype=jnp.int32)
    block_list = jnp.arange(count, dtype=jnp.int32)
    onehot_rows = (row_ids[:, None] // BLOCK == block_list[None, :]).astype(jnp.float32)
    onehot_cols = (col_ids[:, None] // BLOCK == block_list[None, :]).astype(jnp.float32)
    blocks = jnp.maximum(pattern, jnp.eye(count, dtype=jnp.int32)).astype(jnp.float32)
    table = jnp.dot(
        jnp.dot(onehot_rows, blocks, precision=lax.Precision.HIGHEST),
        onehot_cols.T,
        precision=lax.Precision.HIGHEST,
    )
    keep = table > 0.5
    on_diag = row_ids[:, None] == col_ids[None, :]
    shift_here = lax.dynamic_slice_in_dim(shift, row_start, rows_here, 0)
    iterate = (
        jnp.where(keep, matrix.astype(jnp.float32), 0.0)
        + jnp.where(on_diag, shift_here[:, None], 0.0)
    ).astype(jnp.bfloat16)
    column_panel = lax.all_gather(iterate, "col", axis=0, tiled=True)
    row_panel = lax.all_gather(iterate, "row", axis=1, tiled=True)
    full = jnp.dot(row_panel, column_panel, preferred_element_type=jnp.float32)
    full = jnp.where(keep, full, 0.0)
    trace = lax.psum(jnp.sum(jnp.where(on_diag, full, 0.0)), ("row", "col"))
    square = full.astype(jnp.bfloat16)
    gamma = jnp.sqrt(ORDER / jnp.maximum(jnp.abs(trace), 1.0))
    square_panel = lax.all_gather(square, "col", axis=0, tiled=True)
    cube = jnp.dot(row_panel, square_panel, preferred_element_type=jnp.float32)
    cube = jnp.where(keep, cube, 0.0)
    updated = (1.5 * gamma * iterate.astype(jnp.float32) - 0.5 * gamma**3 * cube).astype(
        jnp.bfloat16
    )
    return (square, updated)


def solution(mesh):
    placed = (P("col", "row"), P(), P())
    return jax.shard_map(
        body,
        mesh=mesh,
        in_specs=placed,
        out_specs=(P("col", "row"), P("col", "row")),
        check_vma=False,
    )
```

profile of v0, /device:TPU:1, one launch (start us, length us, event | category | flops | bytes accessed | tf_op | source)
XLA Modules:
  0.0 501.8 jit_solution(705122759896218586)
XLA Ops:
  7.2 0.0 all-gather.4.cloned.1.call-start
  7.3 0.8 dynamic_slice.3
  8.0 1.0 fusion.7
  9.0 2.3 fusion.4
  11.3 0.0 all-gather.4.cloned.1.call-update
  11.3 0.0 all-gather.6.cloned.1.call-start
  11.4 0.7 all-gather.6.cloned.1.call-update
  12.1 0.0 all-gather.8.cloned.1.call-start
  12.1 42.0 %all-gather.4.cloned.1.call-done = bf16[192,6144]{1,0:T(8,128)(2,1)} async-done(((bf16[192,768]{1,0:T(8,128)(2,1)}), bf16[192,6144]{1,0:T(8,128)(2,1)}) %all-gather.4.cloned.1.call-update) | async-done | bytes 2359312 | tf_op jit(solution)/shard_map/all_gather | solution.py:34
  54.1 214.1 %all-gather.6.cloned.1.call-done = bf16[6144,768]{1,0:T(8,128)(2,1)} async-done(((bf16[192,768]{1,0:T(8,128)(2,1)}), bf16[6144,768]{1,0:T(8,128)(2,1)}) %all-gather.6.cloned.1.call-update) | async-done | bytes 9437200 | tf_op jit(solution)/shard_map/all_gather | solution.py:33
  268.2 0.0 copy-start
  268.2 0.0 copy-start.1
  268.2 7.9 %fusion.5 = (f32[]{:T(128)}, bf16[192,768]{1,0:T(8,128)(2,1)}) fusion(s32[768]{0:T(1024)S(1)} %get-tuple-element.8, s32[192]{0:T(256)S(1)} %get-tuple-element.10, pred[192,768]{1,0:T(32,128)(4,1)S(1)} %get-tuple-element.5, bf16[192,6144]{1,0:T(8,128)(2,1)} %all-gather.4.cloned.1.call-done, bf16[6144,768]{1,0:T(8,128)(2,1)} %all-gather.6.cloned.1.call-done), kind=kOutput, calls=%fused_computation.10 | convolution fusion | flops 1812676608 | bytes 12242692 | tf_op jit(solution)/shard_map/dot_general | solution.py:35
  276.1 0.0 all-gather.8.cloned.1.call-update
  276.1 75.1 %psum.7 = f32[]{:T(128)} all-reduce(f32[]{:T(128)} %get-tuple-element.2), channel_id=1, replica_groups=mesh['row'=8,'col'=32] {'row','col'}, use_global_device_ids=true, to_apply=%region_1.2 | all-reduce | flops 1 | bytes 8 | tf_op jit(solution)/shard_map/psum | solution.py:37
  352.0 136.8 %all-gather.8.cloned.1.call-done = bf16[6144,768]{1,0:T(8,128)(2,1)} async-done(((bf16[192,768]{1,0:T(8,128)(2,1)}), bf16[6144,768]{1,0:T(8,128)(2,1)}) %all-gather.8.cloned.1.call-update) | async-done | bytes 9437200 | tf_op jit(solution)/shard_map/all_gather | solution.py:40
  488.8 0.0 copy-done
  488.8 0.0 copy-done.1
  488.8 6.5 %fusion.2 = bf16[192,768]{1,0:T(8,128)(2,1)} fusion(pred[192,768]{1,0:T(32,128)(4,1)S(1)} %get-tuple-element.5, bf16[192,6144]{1,0:T(8,128)(2,1)S(1)} %copy-done.1, bf16[6144,768]{1,0:T(8,128)(2,1)} %all-gather.8.cloned.1.call-done, bf16[192,768]{1,0:T(8,128)(2,1)S(1)} %copy-done, f32[]{:T(128)S(6)} %mul.25, f32[]{:T(128)S(6)} %mul_shard_map.3), kind=kOutput, calls=%fused_computation.4 | convolution fusion | flops 1812824064 | bytes 12533768 | tf_op jit(solution)/shard_map/dot_general | solution.py:41
  (2 shorter events, 0.0 us)
Async XLA Ops:
  7.2 47.0 %all-gather.4.cloned.1.call-start = ((), (), s32[]{:S(2)}) async-start(), calls=%async_computation | async-start | bytes 2654208 | tf_op jit(solution)/shard_map/all_gather | solution.py:34
  11.3 256.9 %all-gather.6.cloned.1.call-start = ((), (), s32[]{:S(2)}) async-start(), calls=%async_computation.1 | async-start | bytes 9732096 | tf_op jit(solution)/shard_map/all_gather | solution.py:33
  12.1 476.8 %all-gather.8.cloned.1.call-start = ((), (), s32[]{:S(2)}) async-start(), calls=%async_computation.2 | async-start | bytes 9732096 | tf_op jit(solution)/shard_map/all_gather | solution.py:40
  268.2 220.6 %copy-start = (bf16[192,768]{1,0:T(8,128)(2,1)S(1)}, bf16[192,768]{1,0:T(8,128)(2,1)}, u32[]{:S(2)}) copy-start(bf16[192,768]{1,0:T(8,128)(2,1)} %get-tuple-element.4) | copy-start | bytes 884740
  268.2 220.6 %copy-start.1 = (bf16[192,6144]{1,0:T(8,128)(2,1)S(1)}, bf16[192,6144]{1,0:T(8,128)(2,1)}, u32[]{:S(2)}) copy-start(bf16[192,6144]{1,0:T(8,128)(2,1)} %all-gather.4.cloned.1.call-done) | copy-start | bytes 7077892
Sparse Core Ops, SparseCore 0:
  11.4 42.6 all-gather.3
  56.5 211.6 all-gather.5
  276.2 212.5 all-gather.7
where the time goes:
time: 502 us
  waiting for transfers between devices  394 us (78%)
  blocking collectives  75.1 us (15%)
  matrix products  17.6 us (4%)
  between operations  14.5 us (3%)
    all_gather x1, waiting for transfers between devices, body(): column_panel = lax.all_gather(iterate, 'col', axis=0, tiled=True)  214 us
    all_gather x1, waiting for transfers between devices, body(): square_panel = lax.all_gather(square, 'col', axis=0, tiled=True)  137 us
    psum x1, blocking collectives, body(): trace = lax.psum(jnp.sum(jnp.where(on_diag, full, 0.0)), ('row', 'col'))  75.1 us
    all_gather x1, waiting for transfers between devices, body(): row_panel = lax.all_gather(iterate, 'row', axis=1, tiled=True)  42 us
  transfers between devices with their start and end apart: 3, of which 3 were waited for; matrix products, arithmetic and copies ran while one was open for 0% of the time, Pallas kernels for 0%

commit v1 on v0

v1 whole, which is shorter than its diff:
```python
import jax
import jax.numpy as jnp
from jax import lax
from jax.experimental import pallas as pl
from jax.experimental.pallas import tpu as pltpu
from jax.sharding import PartitionSpec as P

BLOCK = 128
ORDER = 6144
NBLK = 48
ROWS = 192
COLS = 768
SUB = 64
CHUNK = 256
NCH = COLS // CHUNK
DEPTH = 8 * ROWS
MESH = pl.DeviceIdType.MESH
F32 = jnp.float32
BF16 = jnp.bfloat16


def kernel(m_ref, pat_ref, shift_ref, sq_ref, up_ref,
           g1, g2, zbuf, lhs, part1, part2, got1, got2, acc, tsend, trecv, ssem, rsem, lsem):
    r = lax.axis_index("row")
    c = lax.axis_index("col")
    zhi, core = r // 2, r % 2
    y, x, zlo = c // 8, (c // 2) % 4, c % 2
    me = c % 8

    def dev(dx=0, dy=0, flip=0, dz=0, other=0):
        xx, yy, zz = (x + dx + 4) % 4, (y + dy + 4) % 4, (zhi + dz + 4) % 4
        zl = 1 - zlo if flip else zlo
        cc = 1 - core if other else core
        return (zz * 2 + cc, (yy * 4 + xx) * 2 + zl)

    def place(dx, flip):
        return ((x + dx + 4) % 4) * 2 + (1 - zlo if flip else zlo)

    def rows(slot, start=0, size=ROWS):
        return pl.ds(pl.multiple_of(slot * ROWS + start, 16), size)

    barrier = pltpu.get_barrier_semaphore()
    partners = [dev(dx=1), dev(dx=-1), dev(dy=1), dev(dy=-1), dev(dy=2),
                dev(dz=1), dev(dz=-1), dev(flip=1), dev(other=1)]
    for p in partners:
        pl.semaphore_signal(barrier, inc=1, device_id=p, device_id_type=MESH)

    terms = jnp.zeros((SUB, BLOCK), F32)
    keeps = {}
    for s in range(ROWS // SUB):
        br = (3 * c + s) // 2
        for t in range(COLS // BLOCK):
            bc = 6 * r + t
            diag = br == bc
            keep = jnp.where((pat_ref[br, bc] > 0) | diag, 1.0, 0.0).astype(F32)
            keep_t = jnp.where((pat_ref[bc, br] > 0) | diag, 1.0, 0.0).astype(F32)
            keeps[s, t] = keep
            m = m_ref[s * SUB:(s + 1) * SUB, t * BLOCK:(t + 1) * BLOCK].astype(F32)
            row_ids = c * ROWS + s * SUB + lax.broadcasted_iota(jnp.int32, (SUB, BLOCK), 0)
            col_ids = r * COLS + t * BLOCK + lax.broadcasted_iota(jnp.int32, (SUB, BLOCK), 1)
            on = jnp.where(row_ids == col_ids, shift_ref[pl.ds(bc, 1), :], 0.0)
            a = (m * keep + on).astype(BF16)
            a_t = (m * keep_t + on).astype(BF16)
            terms += a.astype(F32) * a_t.astype(F32)
            k, lane = t // 2, (t % 2) * BLOCK
            g1[k, rows(me, s * SUB, SUB), lane:lane + BLOCK] = a
            zbuf[zhi, s * SUB:(s + 1) * SUB, t * BLOCK:(t + 1) * BLOCK] = a
    tsend[0] = jnp.sum(terms.reshape(SUB // 8, 8, BLOCK), axis=0)

    pl.semaphore_wait(barrier, len(partners))

    index = {}
    started = []

    def number(key):
        if key not in index:
            index[key] = len(index)
        return index[key]

    def copy(key, src, dst, to):
        n = number(key)
        return pltpu.make_async_remote_copy(
            src_ref=src, dst_ref=dst, send_sem=ssem.at[n], recv_sem=rsem.at[n],
            device_id=to, device_id_type=MESH)

    def start(key, src, dst, to):
        op = copy(key, src, dst, to)
        op.start()
        started.append(op)

    def arrived(key, dst):
        copy(key, dst, dst, dev(other=1)).wait_recv()

    def own(g, name, k):
        mine = g.at[k, rows(me), :]
        start((name, "zp", k), mine, mine, dev(flip=1))
        start((name, "xp", k), mine, mine, dev(dx=1))
        start((name, "xm", k), mine, mine, dev(dx=-1))

    def pair(g, name, k):
        ref = g.at[k, rows(place(0, 1)), :]
        arrived((name, "zp", k), ref)
        start((name, "fp", k), ref, ref, dev(dx=1))
        start((name, "fm", k), ref, ref, dev(dx=-1))

    def far(g, name, k, flip):
        first, second = ("fp", "fm") if flip else ("xp", "xm")
        arrived((name, first, k), g.at[k, rows(place(-1, flip)), :])
        ref = g.at[k, rows(place(-1, flip), 0, ROWS // 2), :]
        start((name, "hp", flip, k), ref, ref, dev(dx=1))
        arrived((name, second, k), g.at[k, rows(place(1, flip)), :])
        ref = g.at[k, rows(place(1, flip), ROWS // 2, ROWS // 2), :]
        start((name, "hm", flip, k), ref, ref, dev(dx=-1))

    def last(g, name, k, flip):
        slot = place(2, flip)
        arrived((name, "hp", flip, k), g.at[k, rows(slot, 0, ROWS // 2), :])
        arrived((name, "hm", flip, k), g.at[k, rows(slot, ROWS // 2, ROWS // 2), :])

    half = SUB // 2

    def along_z(q):
        ref = zbuf.at[zhi, pl.ds(q * SUB, SUB), :]
        start(("z+", q), ref, ref, dev(dz=1))
        start(("z-", q), ref, ref, dev(dz=-1))

    def relay_z(q, up):
        if up:
            slot = (zhi + 3) % 4
            arrived(("z+", q), zbuf.at[slot, pl.ds(q * SUB, SUB), :])
            ref = zbuf.at[slot, pl.ds(q * SUB, half), :]
            start(("zz+", q), ref, ref, dev(dz=1))
        else:
            slot = (zhi + 1) % 4
            arrived(("z-", q), zbuf.at[slot, pl.ds(q * SUB, SUB), :])
            ref = zbuf.at[slot, pl.ds(q * SUB + half, half), :]
            start(("zz-", q), ref, ref, dev(dz=-1))

    def relay_last(q):
        slot = (zhi + 2) % 4
        arrived(("zz+", q), zbuf.at[slot, pl.ds(q * SUB, half), :])
        arrived(("zz-", q), zbuf.at[slot, pl.ds(q * SUB + half, half), :])

    core_cols = pl.ds(pl.multiple_of(core * COLS, COLS), COLS)
    sent_y = []

    def along_y(dz, q):
        slot = (zhi + dz + 4) % 4
        d = (slot - y + 4) % 4
        n = number(("ly", dz, q))
        src = zbuf.at[slot, pl.ds(q * SUB, SUB), :]
        dst = lhs.at[rows(y, q * SUB, SUB), core_cols]

        def op():
            return pltpu.make_async_remote_copy(
                src_ref=src, dst_ref=dst, send_sem=ssem.at[n],
                recv_sem=lsem.at[(d + 3) % 4, q],
                device_id=(r, (slot * 4 + x) * 2 + zlo), device_id_type=MESH)

        @pl.when(d != 0)
        def _():
            op().start()

        @pl.when(d == 0)
        def _():
            lhs[rows(y, q * SUB, SUB), core_cols] = zbuf[slot, q * SUB:(q + 1) * SUB, :]

        sent_y.append((d, op))

    def to_core(d):
        slot = (y - d + 4) % 4
        if d:
            for q in range(3):
                ref = lhs.at[rows(slot, q * SUB, SUB), core_cols]
                pltpu.make_async_remote_copy(
                    src_ref=ref, dst_ref=ref, send_sem=ssem.at[0], recv_sem=lsem.at[d - 1, q],
                    device_id=dev(other=1), device_id_type=MESH).wait_recv()
        ref = lhs.at[rows(slot), core_cols]
        start(("lc", d), ref, ref, dev(other=1))

    def from_core(d):
        slot = (y - d + 4) % 4
        cols = pl.ds(pl.multiple_of((1 - core) * COLS, COLS), COLS)
        arrived(("lc", d), lhs.at[rows(slot), cols])

    odd_x, odd_z, odd_y = x % 2, zhi % 2, y % 2
    trace_to = [
        dev(other=1), dev(flip=1),
        dev(dx=1 - 2 * odd_x), dev(dx=2 * odd_x - 1),
        dev(dy=1 - 2 * odd_y), dev(dy=2 * odd_y - 1),
        dev(dz=1 - 2 * odd_z), dev(dz=2 * odd_z - 1),
    ]

    def trace_send(i):
        start(("t", i), tsend.at[i], trecv.at[i], trace_to[i])

    def trace_sum(i):
        arrived(("t", i), trecv.at[i])
        tsend[i + 1] = tsend[i] + trecv[i]
        if i + 1 < len(trace_to):
            trace_send(i + 1)

    def product(g, part, name, k):
        acc[...] = jnp.dot(lhs[...], g[k], preferred_element_type=F32)
        part[k] = acc[...].astype(BF16)
        for d in (2, 1, 3):
            start((name, "rs", d, k), part.at[k, rows((y + d) % 4), :],
                  (got1 if name == "a" else got2).at[k, d - 1], dev(dy=d))

    def total(got, name, k, mine):
        for d in (1, 3, 2):
            arrived((name, "rs", d, k), got.at[k, d - 1])
        return mine + (got[k, 0].astype(F32) + got[k, 2].astype(F32)) + got[k, 1].astype(F32)

    for k in range(NCH):
        own(g1, "a", k)
        along_z(k)
    for q in range(3):
        along_y(0, q)
    trace_send(0)
    for k in range(NCH):
        pair(g1, "a", k)
        far(g1, "a", k, 0)
        relay_z(k, True)
        relay_z(k, False)
        along_y(-1, k)
        along_y(1, k)
    trace_sum(0)
    for k in range(NCH):
        far(g1, "a", k, 1)
    trace_sum(1)
    for q in range(3):
        relay_last(q)
        along_y(2, q)
    trace_sum(2)
    for d in (0, 1, 3, 2):
        to_core(d)
    for k in range(NCH):
        last(g1, "a", k, 0)
        last(g1, "a", k, 1)
    for d in (0, 1, 3, 2):
        from_core(d)

    def mine():
        return acc[rows(y), :]

    held = []
    for k in range(NCH):
        product(g1, part1, "a", k)
        held.append(mine())
    trace_sum(3)
    for k in range(NCH):
        full = total(got1, "a", k, held[k])
        for s in range(ROWS // SUB):
            for h in range(2):
                t = 2 * k + h
                piece = full[s * SUB:(s + 1) * SUB, h * BLOCK:(h + 1) * BLOCK] * keeps[s, t]
                piece = piece.astype(BF16)
                g2[k, rows(me, s * SUB, SUB), h * BLOCK:(h + 1) * BLOCK] = piece
                sq_ref[s * SUB:(s + 1) * SUB, t * BLOCK:(t + 1) * BLOCK] = piece
        own(g2, "b", k)
        if k:
            pair(g2, "b", k - 1)
            far(g2, "b", k - 1, 0)
    trace_sum(4)
    pair(g2, "b", NCH - 1)
    far(g2, "b", 0, 1)
    far(g2, "b", NCH - 1, 0)
    trace_sum(5)
    far(g2, "b", 1, 1)
    last(g2, "b", 0, 0)
    last(g2, "b", 0, 1)
    held = []
    product(g2, part2, "b", 0)
    held.append(mine())
    trace_sum(6)
    far(g2, "b", 2, 1)
    last(g2, "b", 1, 0)
    last(g2, "b", 1, 1)
    product(g2, part2, "b", 1)
    held.append(mine())
    trace_sum(7)
    last(g2, "b", 2, 0)
    last(g2, "b", 2, 1)
    product(g2, part2, "b", 2)
    held.append(mine())

    trace = jnp.sum(tsend[len(trace_to)], keepdims=True)
    gamma = jnp.sqrt(ORDER / jnp.maximum(jnp.abs(trace), 1.0))
    lead, tail = 1.5 * gamma, 0.5 * gamma * gamma * gamma
    for k in range(NCH):
        cube = total(got2, "b", k, held[k])
        for s in range(ROWS // SUB):
            for h in range(2):
                t = 2 * k + h
                piece = cube[s * SUB:(s + 1) * SUB, h * BLOCK:(h + 1) * BLOCK] * keeps[s, t]
                a = zbuf[zhi, s * SUB:(s + 1) * SUB, t * BLOCK:(t + 1) * BLOCK].astype(F32)
                up_ref[s * SUB:(s + 1) * SUB, t * BLOCK:(t + 1) * BLOCK] = (
                    lead * a - tail * piece).astype(BF16)

    for op in started:
        op.wait_send()
    for d, op in sent_y:
        @pl.when(d != 0)
        def _(op=op):
            op().wait_send()


NSEM = 128


def body(matrix, pattern, shift):
    block = jax.ShapeDtypeStruct((ROWS, COLS), BF16)
    vmem = pl.BlockSpec(memory_space=pltpu.VMEM)
    return pl.pallas_call(
        kernel,
        out_shape=(block, block),
        in_specs=[vmem, pl.BlockSpec(memory_space=pltpu.SMEM), vmem],
        out_specs=(vmem, vmem),
        scratch_shapes=[
            pltpu.VMEM((NCH, DEPTH, CHUNK), BF16),
            pltpu.VMEM((NCH, DEPTH, CHUNK), BF16),
            pltpu.VMEM((4, ROWS, COLS), BF16),
            pltpu.VMEM((4 * ROWS, DEPTH), BF16),
            pltpu.VMEM((NCH, 4 * ROWS, CHUNK), BF16),
            pltpu.VMEM((NCH, 4 * ROWS, CHUNK), BF16),
            pltpu.VMEM((NCH, 3, ROWS, CHUNK), BF16),
            pltpu.VMEM((NCH, 3, ROWS, CHUNK), BF16),
            pltpu.VMEM((4 * ROWS, CHUNK), F32),
            pltpu.VMEM((9, 8, BLOCK), F32),
            pltpu.VMEM((8, 8, BLOCK), F32),
            pltpu.SemaphoreType.DMA((NSEM,)),
            pltpu.SemaphoreType.DMA((NSEM,)),
            pltpu.SemaphoreType.DMA((3, 3)),
        ],
        compiler_params=pltpu.CompilerParams(
            collective_id=0, has_side_effects=True, vmem_limit_bytes=40 * 2**20),
        cost_estimate=pl.CostEstimate(
            flops=4 * ROWS * COLS * ORDER, bytes_accessed=6 * ROWS * COLS, transcendentals=0),
        name="sign_step",
    )(matrix, pattern, shift.reshape(NBLK, BLOCK))


def solution(mesh):
    placed = (P("col", "row"), P(), P())
    return jax.shard_map(
        body,
        mesh=mesh,
        in_specs=placed,
        out_specs=(P("col", "row"), P("col", "row")),
        check_vma=False,
    )
```

time: 502 us -> 108 us (0.22)
  waiting for transfers between devices: 394 us -> 0 us
  Pallas kernels: 0 us -> 104 us
  blocking collectives: 75.1 us -> 0 us
  matrix products: 17.6 us -> 0 us
  between operations: 14.5 us -> 0.65 us
    all_gather x3 -> x0, waiting for transfers between devices: 393 us -> none  [the longest x1 214 us: body(): column_panel = lax.all_gather(iterate, 'col', axis=0, tiled=True)]
    pallas_call x0 -> x1, Pallas kernels: none -> 104 us  [body(): pl.pallas_call(kernel, out_shape=(block, block), in_specs=[vmem, pl.Block...]
    psum x1 -> x0, blocking collectives: 75.1 us -> none  [body(): trace = lax.psum(jnp.sum(jnp.where(on_diag, full, 0.0)), ('row', 'col'))]
    dot_general x4 -> x0, matrix products: 17.6 us -> none  [the longest x1 7.88 us: body(): full = jnp.dot(row_panel, column_panel, preferred_element_type=jnp.float32)]
  transfers between devices with their start and end apart: 3 -> 0, of which waited for: 3 -> 0; matrix products, arithmetic and copies ran while one was open for 0% -> 0% of each run, Pallas kernels for 0% -> 0%
where the time goes in v1:
time: 108 us
  Pallas kernels  104 us (96%)
  local copies, waits for them, and re-layouts  3.86 us (4%)
    pallas_call x1, Pallas kernels, body(): pl.pallas_call(kernel, out_shape=(block, block), in_specs=[vmem, pl.Block...  104 us
    unnamed x8, local copies, waits for them, and re-layouts  3.86 us

profile of v1, /device:TPU:1, one launch (start us, length us, event | category | flops | bytes accessed | tf_op | source)
XLA Modules:
  0.0 108.0 jit_solution(5463817371720656529)
XLA Ops:
  0.6 0.0 copy-start
  0.6 1.0 copy-done
  1.6 0.0 copy-start.1
  1.6 0.7 copy-done.1
  2.3 0.0 copy-start.2
  2.3 0.7 copy-done.2
  3.1 103.5 %sign_step.1 = (bf16[192,768]{1,0:T(8,128)(2,1)S(1)}, bf16[192,768]{1,0:T(8,128)(2,1)S(1)}) custom-call(bf16[192,768]{1,0:T(8,128)(2,1)S(1)} %copy-done, s32[48,48]{1,0:T(8,128)S(1)} %copy-done.1, f32[48,128]{1,0:T(8,128)S(1)} %bitcast.1), custom_call_target="tpu_custom_call" | custom-call | flops 3623878656 | bytes 884736 | tf_op jit(solution)/shard_map/sign_step/pallas_call | solution.py:315
  106.6 0.7 copy.7
  107.3 0.7 copy.8
Async XLA Ops:
  0.6 1.0 copy-start
  1.6 0.7 copy-start.1
  2.3 0.7 copy-start.2

commit v2 on v0

v2 whole, which is shorter than its diff:
```python
import jax
import jax.numpy as jnp
from jax import lax
from jax.experimental import pallas as pl
from jax.experimental.pallas import tpu as pltpu
from jax.sharding import PartitionSpec as P

BLOCK = 128
ORDER = 6144
NBLK = 48
ROWS = 192
COLS = 768
WIDE = COLS // 2
SUB = 64
CHUNK = 256
NCH = COLS // CHUNK
DEPTH = 8 * ROWS
NQ = 2
PIECE = ROWS // NQ
NSEM = 80
MESH = pl.DeviceIdType.MESH
F32 = jnp.float32
BF16 = jnp.bfloat16


def kernel(m_ref, pat_ref, shift_ref, sq_ref, up_ref,
           g1, g2, zbuf, lhs, part1, part2, got1, got2, own1, own2, acc, tsend, trecv, sems):
    r = lax.axis_index("row")
    c = lax.axis_index("col")
    zhi, core = lax.div(r, 2), lax.rem(r, 2)
    y, x, zlo = lax.div(c, 8), lax.rem(lax.div(c, 2), 4), lax.rem(c, 2)
    me = y * 2 + zlo

    ys = {d: lax.rem(y + d, 4) for d in range(1, 4)}
    xs = {d: lax.rem(x + d, 4) for d in range(1, 4)}
    zs = {d: lax.rem(zhi + d, 4) for d in range(1, 4)}
    ys[0], xs[0], zs[0] = y, x, zhi
    y_up, y_down = (r, c + 8 * (ys[1] - y)), (r, c + 8 * (ys[3] - y))
    z_up, z_down = (r + 2 * (zs[1] - zhi), c), (r + 2 * (zs[3] - zhi), c)
    pair_dev = (r, c + 1 - 2 * zlo)
    core_dev = (r + 1 - 2 * core, c)
    x_dev = {d: (r, c + 2 * (xs[d] - x)) for d in range(1, 4)}

    def rows(slot, start=0, size=ROWS):
        return pl.ds(pl.multiple_of(slot * ROWS + start, 16), size)

    barrier = pltpu.get_barrier_semaphore()
    partners = [x_dev[1], x_dev[2], x_dev[3], y_up, y_down, z_up, z_down, pair_dev, core_dev]
    for p in partners:
        pl.semaphore_signal(barrier, inc=1, device_id=p, device_id_type=MESH)

    terms = jnp.zeros((SUB, BLOCK), F32)
    keeps = {}
    ahead = (lax.broadcasted_iota(jnp.int32, (SUB, BLOCK), 0)
             - lax.broadcasted_iota(jnp.int32, (SUB, BLOCK), 1))
    for s in range(ROWS // SUB):
        br = lax.div(3 * c + s, 2)
        for t in range(COLS // BLOCK):
            bc = 6 * r + t
            diag = br == bc
            keep = jnp.where((pat_ref[br, bc] > 0) | diag, 1.0, 0.0).astype(F32)
            keep_t = jnp.where((pat_ref[bc, br] > 0) | diag, 1.0, 0.0).astype(F32)
            keeps[s, t] = keep
            m = m_ref[s * SUB:(s + 1) * SUB, t * BLOCK:(t + 1) * BLOCK].astype(F32)
            gap = (r * COLS + t * BLOCK) - (c * ROWS + s * SUB)
            on = jnp.where(ahead == gap, shift_ref[pl.ds(bc, 1), :], 0.0)
            a = (m * keep + on).astype(BF16)
            a_t = (m * keep_t + on).astype(BF16)
            terms += a.astype(F32) * a_t.astype(F32)
            k, lane = t // 2, (t % 2) * BLOCK
            g1[k, rows(me, s * SUB, SUB), lane:lane + BLOCK] = a
            zbuf[zhi, t // 3, s * SUB:(s + 1) * SUB, (t % 3) * BLOCK:(t % 3 + 1) * BLOCK] = a
    tsend[0] = jnp.sum(terms.reshape(SUB // 8, 8, BLOCK), axis=0)

    pl.semaphore_wait(barrier, len(partners))

    index = {}

    def sem(key):
        if key not in index:
            index[key] = len(index)
        return sems.at[index[key]]

    def copy(out, into, src, dst, to):
        return pltpu.make_async_remote_copy(
            src_ref=src, dst_ref=dst, send_sem=sem(out), recv_sem=sem(into),
            device_id=to, device_id_type=MESH)

    def start(out, into, ref, to, dst=None):
        copy(out, into, ref, ref if dst is None else dst, to).start()

    def arrived(key, ref):
        copy(key, key, ref, ref, core_dev).wait_recv()

    def sent(key, ref):
        copy(key, key, ref, ref, core_dev).wait_send()

    slots = {(d, f): rows(ys[d] * 2 + (1 - zlo if f else zlo)) for d in range(4) for f in range(2)}
    tops = {(d, f): rows(ys[d] * 2 + (1 - zlo if f else zlo), 0, ROWS // 2)
            for d in range(4) for f in range(2)}
    ends = {(d, f): rows(ys[d] * 2 + (1 - zlo if f else zlo), ROWS // 2, ROWS // 2)
            for d in range(4) for f in range(2)}

    def own(g, name, k):
        ref = g.at[k, slots[0, 0], :]
        start((name, "out"), (name, "pair", k), ref, pair_dev)
        start((name, "out"), (name, "near", 0, k), ref, y_up)
        start((name, "out"), (name, "near", 0, k), ref, y_down)

    def pair(g, name, k):
        ref = g.at[k, slots[0, 1], :]
        arrived((name, "pair", k), ref)
        start((name, "out"), (name, "near", 1, k), ref, y_up)
        start((name, "out"), (name, "near", 1, k), ref, y_down)

    def near(g, name, k, f):
        arrived((name, "near", f, k), g.at[k, 0:2 * ROWS, :])

    def relay(g, name, k, f):
        near(g, name, k, f)
        start((name, "out"), (name, "far", f, k), g.at[k, tops[3, f], :], y_up)
        start((name, "out"), (name, "far", f, k), g.at[k, ends[1, f], :], y_down)

    def far(g, name, k, f):
        arrived((name, "far", f, k), g.at[k, slots[2, f], :])

    def far_pair(g, name, k):
        far(g, name, k, 0)
        start((name, "out"), (name, "far", 1, k), g.at[k, slots[2, 0], :], pair_dev)

    def along_z(q):
        ref = zbuf.at[zhi, :, q * PIECE:(q + 1) * PIECE, :]
        start(("z", "out"), ("z", q), ref, z_up)
        start(("z", "out"), ("z", q), ref, z_down)

    def relay_z(q):
        arrived(("z", q), zbuf.at[0:2, :, 0:PIECE, :])
        low, mid, high = q * PIECE, q * PIECE + PIECE // 2, (q + 1) * PIECE
        start(("z", "out"), ("zz", q), zbuf.at[zs[3], :, low:mid, :], z_up)
        start(("z", "out"), ("zz", q), zbuf.at[zs[1], :, mid:high, :], z_down)

    def relay_last(q):
        arrived(("zz", q), zbuf.at[zs[2], :, q * PIECE:(q + 1) * PIECE, :])

    direct = core == lax.div(x, 2)
    depth = {d: pl.ds(pl.multiple_of(zs[d] * WIDE, BLOCK), WIDE) for d in range(4)}
    to_x = [core * 2 + h for h in range(2)]
    home = lax.rem(x, 2)

    def along_x(d, q):
        dst = lhs.at[rows(x, q * PIECE, PIECE), depth[d]]
        for h in range(2):
            src = zbuf.at[zs[d], h, q * PIECE:(q + 1) * PIECE, :]

            @pl.when(to_x[h] != x)
            def _(h=h, src=src):
                start(("x", "out"), ("x", d), src, (r, c + 2 * (to_x[h] - x)), dst)

            @pl.when(to_x[h] == x)
            def _(h=h):
                lhs[rows(x, q * PIECE, PIECE), depth[d]] = zbuf[
                    zs[d], h, q * PIECE:(q + 1) * PIECE, :]

    def to_core(d):
        ref = lhs.at[:, depth[d]]

        @pl.when(direct)
        def _():
            arrived(("x", d), lhs.at[0:3 * ROWS, depth[d]])
            start(("core", "out"), ("core", d), ref, core_dev)

    def from_core(d):
        @pl.when(jnp.logical_not(direct))
        def _():
            arrived(("core", d), lhs.at[:, depth[d]])

    odd_x, odd_z, odd_y = lax.rem(x, 2), lax.rem(zhi, 2), lax.rem(y, 2)

    def step(first, d1, d3):
        return tuple(jnp.where(first, u, v) for u, v in zip(d1, d3))

    trace_to = [
        core_dev, pair_dev,
        step(odd_x == 0, x_dev[1], x_dev[3]), step(odd_x == 1, x_dev[1], x_dev[3]),
        step(odd_y == 0, y_up, y_down), step(odd_y == 1, y_up, y_down),
        step(odd_z == 0, z_up, z_down), step(odd_z == 1, z_up, z_down),
    ]

    def trace_send(i):
        start(("t", "out"), ("t", i), tsend.at[i], trace_to[i], trecv.at[i])

    def trace_sum(i):
        arrived(("t", i), trecv.at[i])
        tsend[i + 1] = tsend[i] + trecv[i]
        if i + 1 < len(trace_to):
            trace_send(i + 1)

    def part_dot(g, k, slot, first=False):
        term = jnp.dot(lhs[:, pl.ds(pl.multiple_of(slot * WIDE, BLOCK), WIDE)],
                       g[k, pl.ds(pl.multiple_of(slot * WIDE, 16), WIDE), :],
                       preferred_element_type=F32)
        acc[k] = term if first else acc[k] + term

    def ship(part, kept, got, name, k):
        for d in (2, 1, 3):
            part[k, d - 1] = acc[k, rows(xs[d]), :].astype(BF16)
        kept[k] = acc[k, rows(x), :]
        if k:
            sent((name, "sums out", k - 1), part.at[k - 1])
        for d in (2, 1, 3):
            start((name, "sums out", k), (name, "sums", k), part.at[k, d - 1], x_dev[d],
                  got.at[k, d - 1])

    def total(got, kept, name, k):
        arrived((name, "sums", k), got.at[k])
        return kept[k] + (got[k, 0].astype(F32) + got[k, 2].astype(F32)) + got[k, 1].astype(F32)

    for k in range(NCH):
        own(g1, "a", k)
    for q in range(NQ):
        along_x(0, q)
    trace_send(0)
    pair(g1, "a", 0)
    along_z(0)
    relay(g1, "a", 0, 0)
    pair(g1, "a", 1)
    along_z(1)
    relay(g1, "a", 1, 0)
    pair(g1, "a", 2)
    relay(g1, "a", 2, 0)
    relay_z(0)
    along_x(3, 0)
    along_x(1, 0)
    trace_sum(0)
    relay(g1, "a", 0, 1)
    relay_z(1)
    along_x(3, 1)
    along_x(1, 1)
    trace_sum(1)
    relay(g1, "a", 1, 1)
    relay(g1, "a", 2, 1)
    to_core(0)
    relay_last(0)
    along_x(2, 0)
    to_core(3)
    to_core(1)
    for k in range(NCH):
        far(g1, "a", k, 0)
        far(g1, "a", k, 1)
    for d in (0, 3, 1):
        from_core(d)
        if d == 3:
            relay_last(1)
            along_x(2, 1)
        for k in range(NCH):
            part_dot(g1, k, zs[d], d == 0)
    to_core(2)
    from_core(2)
    for k in range(NCH):
        part_dot(g1, k, zs[2])
        ship(part1, own1, got1, "a", k)
    def squares(k):
        full = total(got1, own1, "a", k)
        for s in range(ROWS // SUB):
            for h in range(2):
                t = 2 * k + h
                piece = full[s * SUB:(s + 1) * SUB, h * BLOCK:(h + 1) * BLOCK] * keeps[s, t]
                piece = piece.astype(BF16)
                g2[k, rows(me, s * SUB, SUB), h * BLOCK:(h + 1) * BLOCK] = piece
                sq_ref[s * SUB:(s + 1) * SUB, t * BLOCK:(t + 1) * BLOCK] = piece
        own(g2, "b", k)

    squares(0)
    trace_sum(2)
    pair(g2, "b", 0)
    relay(g2, "b", 0, 0)
    squares(1)
    trace_sum(3)
    far_pair(g2, "b", 0)
    pair(g2, "b", 1)
    relay(g2, "b", 1, 0)
    part_dot(g2, 0, ys[0], True)
    squares(2)
    trace_sum(4)
    near(g2, "b", 0, 1)
    part_dot(g2, 0, ys[1])
    part_dot(g2, 0, ys[3])
    far_pair(g2, "b", 1)
    part_dot(g2, 1, ys[0], True)
    pair(g2, "b", 2)
    relay(g2, "b", 2, 0)
    far(g2, "b", 0, 1)
    part_dot(g2, 0, ys[2])
    ship(part2, own2, got2, "b", 0)
    near(g2, "b", 1, 1)
    part_dot(g2, 1, ys[1])
    part_dot(g2, 1, ys[3])
    far_pair(g2, "b", 2)
    part_dot(g2, 2, ys[0], True)
    far(g2, "b", 1, 1)
    part_dot(g2, 1, ys[2])
    trace_sum(5)
    ship(part2, own2, got2, "b", 1)
    near(g2, "b", 2, 1)
    part_dot(g2, 2, ys[1])
    part_dot(g2, 2, ys[3])
    trace_sum(6)
    far(g2, "b", 2, 1)
    part_dot(g2, 2, ys[2])
    ship(part2, own2, got2, "b", 2)
    trace_sum(7)

    trace = jnp.sum(tsend[len(trace_to)], keepdims=True)
    gamma = jnp.sqrt(ORDER / jnp.maximum(jnp.abs(trace), 1.0))
    lead, tail = 1.5 * gamma, 0.5 * gamma * gamma * gamma
    for k in range(NCH):
        cube = total(got2, own2, "b", k)
        for s in range(ROWS // SUB):
            for h in range(2):
                t = 2 * k + h
                piece = cube[s * SUB:(s + 1) * SUB, h * BLOCK:(h + 1) * BLOCK] * keeps[s, t]
                a = g1[k, rows(me, s * SUB, SUB), h * BLOCK:(h + 1) * BLOCK].astype(F32)
                up_ref[s * SUB:(s + 1) * SUB, t * BLOCK:(t + 1) * BLOCK] = (
                    lead * a - tail * piece).astype(BF16)

    for g, name, part in ((g1, "a", part1), (g2, "b", part2)):
        sent((name, "out"), g.at[:, 0:7 * ROWS, :])
        sent((name, "sums out", NCH - 1), part.at[NCH - 1])
    sent(("z", "out"), zbuf.at[0:3])
    sent(("t", "out"), tsend.at[0:len(trace_to)])

    @pl.when(direct)
    def _():
        sent(("x", "out"), zbuf.at[:, 0])
        sent(("core", "out"), lhs)

    @pl.when(jnp.logical_not(direct))
    def _():
        sent(("x", "out"), zbuf)


def body(matrix, pattern, shift):
    block = jax.ShapeDtypeStruct((ROWS, COLS), BF16)
    vmem = pl.BlockSpec(memory_space=pltpu.VMEM)
    return pl.pallas_call(
        kernel,
        out_shape=(block, block),
        in_specs=[vmem, pl.BlockSpec(memory_space=pltpu.SMEM), vmem],
        out_specs=(vmem, vmem),
        scratch_shapes=[
            pltpu.VMEM((NCH, DEPTH, CHUNK), BF16),
            pltpu.VMEM((NCH, DEPTH, CHUNK), BF16),
            pltpu.VMEM((4, 2, ROWS, WIDE), BF16),
            pltpu.VMEM((4 * ROWS, DEPTH), BF16),
            pltpu.VMEM((NCH, 3, ROWS, CHUNK), BF16),
            pltpu.VMEM((NCH, 3, ROWS, CHUNK), BF16),
            pltpu.VMEM((NCH, 3, ROWS, CHUNK), BF16),
            pltpu.VMEM((NCH, 3, ROWS, CHUNK), BF16),
            pltpu.VMEM((NCH, ROWS, CHUNK), F32),
            pltpu.VMEM((NCH, ROWS, CHUNK), F32),
            pltpu.VMEM((NCH, 4 * ROWS, CHUNK), F32),
            pltpu.VMEM((9, 8, BLOCK), F32),
            pltpu.VMEM((8, 8, BLOCK), F32),
            pltpu.SemaphoreType.DMA((NSEM,)),
        ],
        compiler_params=pltpu.CompilerParams(
            collective_id=0, has_side_effects=True, vmem_limit_bytes=40 * 2**20),
        cost_estimate=pl.CostEstimate(
            flops=4 * ROWS * COLS * ORDER, bytes_accessed=6 * ROWS * COLS, transcendentals=0),
        name="sign_step",
    )(matrix, pattern, shift.reshape(NBLK, BLOCK))


def solution(mesh):
    placed = (P("col", "row"), P(), P())
    return jax.shard_map(
        body,
        mesh=mesh,
        in_specs=placed,
        out_specs=(P("col", "row"), P("col", "row")),
        check_vma=False,
    )
```

time: 502 us -> 94.6 us (0.19)
  waiting for transfers between devices: 394 us -> 0 us
  Pallas kernels: 0 us -> 88.3 us
  blocking collectives: 75.1 us -> 0 us
  matrix products: 17.6 us -> 0 us
  between operations: 14.5 us -> 0.65 us
    all_gather x3 -> x0, waiting for transfers between devices: 393 us -> none  [the longest x1 214 us: body(): column_panel = lax.all_gather(iterate, 'col', axis=0, tiled=True)]
    pallas_call x0 -> x1, Pallas kernels: none -> 88.3 us  [body(): pl.pallas_call(kernel, out_shape=(block, block), in_specs=[vmem, pl.Block...]
    psum x1 -> x0, blocking collectives: 75.1 us -> none  [body(): trace = lax.psum(jnp.sum(jnp.where(on_diag, full, 0.0)), ('row', 'col'))]
    dot_general x4 -> x0, matrix products: 17.6 us -> none  [the longest x1 7.88 us: body(): full = jnp.dot(row_panel, column_panel, preferred_element_type=jnp.float32)]
  transfers between devices with their start and end apart: 3 -> 0, of which waited for: 3 -> 0; matrix products, arithmetic and copies ran while one was open for 0% -> 0% of each run, Pallas kernels for 0% -> 0%
where the time goes in v2:
time: 94.6 us; the launch traced here: 92.8 us
  Pallas kernels  88.3 us (93%)
  local copies, waits for them, and re-layouts  3.86 us (4%)
    pallas_call x1, Pallas kernels, body(): pl.pallas_call(kernel, out_shape=(block, block), in_specs=[vmem, pl.Block...  88.3 us
    unnamed x8, local copies, waits for them, and re-layouts  3.86 us

profile of v2, /device:TPU:1, one launch (start us, length us, event | category | flops | bytes accessed | tf_op | source)
XLA Modules:
  0.0 92.8 jit_solution(8771216867605252172)
XLA Ops:
  0.6 0.0 copy-start
  0.6 1.0 %copy-done = bf16[192,768]{1,0:T(8,128)(2,1)S(1)} copy-done((bf16[192,768]{1,0:T(8,128)(2,1)S(1)}, bf16[192,768]{1,0:T(8,128)(2,1)}, u32[]{:S(2)}) %copy-start) | copy-done | bytes 294936
  1.6 0.0 copy-start.1
  1.6 0.7 copy-done.1
  2.3 0.0 copy-start.2
  2.3 0.7 copy-done.2
  3.1 88.3 %sign_step.1 = (bf16[192,768]{1,0:T(8,128)(2,1)S(1)}, bf16[192,768]{1,0:T(8,128)(2,1)S(1)}) custom-call(bf16[192,768]{1,0:T(8,128)(2,1)S(1)} %copy-done, s32[48,48]{1,0:T(8,128)S(1)} %copy-done.1, f32[48,128]{1,0:T(8,128)S(1)} %bitcast.1), custom_call_target="tpu_custom_call" | custom-call | flops 3623878656 | bytes 884736 | tf_op jit(solution)/shard_map/sign_step/pallas_call | solution.py:345
  91.4 0.7 copy.7
  92.1 0.7 copy.8
Async XLA Ops:
  0.6 1.0 %copy-start = (bf16[192,768]{1,0:T(8,128)(2,1)S(1)}, bf16[192,768]{1,0:T(8,128)(2,1)}, u32[]{:S(2)}) copy-start(bf16[192,768]{1,0:T(8,128)(2,1)} %m_ref.1) | copy-start | bytes 884740
  1.6 0.7 copy-start.1
  2.3 0.7 copy-start.2

commit v3 on v2

--- a/solution.py
+++ b/solution.py
@@ -15,16 +15,17 @@
 CHUNK = 256
 NCH = COLS // CHUNK
 DEPTH = 8 * ROWS
-NQ = 2
+NQ = 3
 PIECE = ROWS // NQ
-NSEM = 80
+BAND = 4 * PIECE
+NSEM = 81
 MESH = pl.DeviceIdType.MESH
 F32 = jnp.float32
 BF16 = jnp.bfloat16
 
 
-def kernel(m_ref, pat_ref, shift_ref, sq_ref, up_ref,
-           g1, g2, zbuf, lhs, part1, part2, got1, got2, own1, own2, acc, tsend, trecv, sems):
+def kernel(m_hbm, pat_ref, shift_hbm, sq_ref, up_ref,
+           m_ref, shift_ref, g1, g2, zbuf, lhs, part1, part2, got1, got2, own1, own2, acc, tsend, trecv, sems):
     r = lax.axis_index("row")
     c = lax.axis_index("col")
     zhi, core = lax.div(r, 2), lax.rem(r, 2)
@@ -44,10 +45,18 @@
     def rows(slot, start=0, size=ROWS):
         return pl.ds(pl.multiple_of(slot * ROWS + start, 16), size)
 
+    loads = [pltpu.make_async_copy(m_hbm, m_ref, sems.at[NSEM]),
+             pltpu.make_async_copy(shift_hbm, shift_ref, sems.at[NSEM + 1])]
+    for load in loads:
+        load.start()
+
     barrier = pltpu.get_barrier_semaphore()
     partners = [x_dev[1], x_dev[2], x_dev[3], y_up, y_down, z_up, z_down, pair_dev, core_dev]
     for p in partners:
         pl.semaphore_signal(barrier, inc=1, device_id=p, device_id_type=MESH)
+
+    for load in loads:
+        load.wait()
 
     terms = jnp.zeros((SUB, BLOCK), F32)
     keeps = {}
@@ -133,46 +142,47 @@
         start(("z", "out"), ("z", q), ref, z_up)
         start(("z", "out"), ("z", q), ref, z_down)
 
-    def relay_z(q):
-        arrived(("z", q), zbuf.at[0:2, :, 0:PIECE, :])
-        low, mid, high = q * PIECE, q * PIECE + PIECE // 2, (q + 1) * PIECE
-        start(("z", "out"), ("zz", q), zbuf.at[zs[3], :, low:mid, :], z_up)
-        start(("z", "out"), ("zz", q), zbuf.at[zs[1], :, mid:high, :], z_down)
-
-    def relay_last(q):
-        arrived(("zz", q), zbuf.at[zs[2], :, q * PIECE:(q + 1) * PIECE, :])
-
     direct = core == lax.div(x, 2)
     depth = {d: pl.ds(pl.multiple_of(zs[d] * WIDE, BLOCK), WIDE) for d in range(4)}
     to_x = [core * 2 + h for h in range(2)]
     home = lax.rem(x, 2)
 
     def along_x(d, q):
-        dst = lhs.at[rows(x, q * PIECE, PIECE), depth[d]]
+        into = pl.ds(pl.multiple_of(q * BAND + x * PIECE, 16), PIECE)
+        dst = lhs.at[into, depth[d]]
         for h in range(2):
             src = zbuf.at[zs[d], h, q * PIECE:(q + 1) * PIECE, :]
 
             @pl.when(to_x[h] != x)
             def _(h=h, src=src):
-                start(("x", "out"), ("x", d), src, (r, c + 2 * (to_x[h] - x)), dst)
+                start(("x", "out"), ("x", d, q), src, (r, c + 2 * (to_x[h] - x)), dst)
 
             @pl.when(to_x[h] == x)
             def _(h=h):
-                lhs[rows(x, q * PIECE, PIECE), depth[d]] = zbuf[
-                    zs[d], h, q * PIECE:(q + 1) * PIECE, :]
-
-    def to_core(d):
-        ref = lhs.at[:, depth[d]]
+                lhs[into, depth[d]] = zbuf[zs[d], h, q * PIECE:(q + 1) * PIECE, :]
+
+    def relay_z(q):
+        arrived(("z", q), zbuf.at[0:2, :, 0:PIECE, :])
+        half = PIECE // 2
+        for back, row, first in ((3, z_up[0], 0), (1, z_down[0], half)):
+            into = pl.ds(pl.multiple_of(q * BAND + x * PIECE + first, 16), half)
+            low = q * PIECE + first
+            for h in range(2):
+                start(("z", "out"), ("x", 2, q), zbuf.at[zs[back], h, low:low + half, :],
+                      (row, c + 2 * (to_x[h] - x)), lhs.at[into, depth[back]])
+
+    def to_core(d, q):
+        ref = lhs.at[q * BAND:(q + 1) * BAND, depth[d]]
 
         @pl.when(direct)
         def _():
-            arrived(("x", d), lhs.at[0:3 * ROWS, depth[d]])
-            start(("core", "out"), ("core", d), ref, core_dev)
-
-    def from_core(d):
+            arrived(("x", d, q), lhs.at[0:(4 if d == 2 else 3) * PIECE, depth[d]])
+            start(("core", "out"), ("core", d, q), ref, core_dev)
+
+    def from_core(d, q):
         @pl.when(jnp.logical_not(direct))
         def _():
-            arrived(("core", d), lhs.at[:, depth[d]])
+            arrived(("core", d, q), lhs.at[q * BAND:(q + 1) * BAND, depth[d]])
 
     odd_x, odd_z, odd_y = lax.rem(x, 2), lax.rem(zhi, 2), lax.rem(y, 2)
 
@@ -195,70 +205,106 @@
         if i + 1 < len(trace_to):
             trace_send(i + 1)
 
-    def part_dot(g, k, slot, first=False):
-        term = jnp.dot(lhs[:, pl.ds(pl.multiple_of(slot * WIDE, BLOCK), WIDE)],
-                       g[k, pl.ds(pl.multiple_of(slot * WIDE, 16), WIDE), :],
-                       preferred_element_type=F32)
-        acc[k] = term if first else acc[k] + term
-
-    def ship(part, kept, got, name, k):
+    def span(slot):
+        return pl.ds(pl.multiple_of(slot * WIDE, BLOCK), WIDE)
+
+    def part_dot(g, k, slot, first=False, band=None):
+        band = pl.ds(0, 4 * ROWS) if band is None else band
+        term = jnp.dot(lhs[band, span(slot)], g[k, span(slot), :], preferred_element_type=F32)
+        acc[k, band] = term if first else acc[k, band] + term
+
+    def piece(k, q, d):
+        return acc[k, pl.ds(pl.multiple_of(q * BAND + xs[d] * PIECE, 16), PIECE), :]
+
+    def ship_band(k, q):
+        band = pl.ds(q * PIECE, PIECE)
         for d in (2, 1, 3):
-            part[k, d - 1] = acc[k, rows(xs[d]), :].astype(BF16)
-        kept[k] = acc[k, rows(x), :]
+            part1[k, d - 1, band] = piece(k, q, d).astype(BF16)
+            start(("a", "sums out"), ("a", "sums", k), part1.at[k, d - 1, band, :], x_dev[d],
+                  got1.at[k, d - 1, band, :])
+        own1[k, band] = piece(k, q, 0)
+
+    def early(q):
+        band = pl.ds(q * BAND, BAND)
+        for k in range(NCH):
+            acc[k, band] = jnp.dot(lhs[band, :], g1[k], preferred_element_type=F32)
+            ship_band(k, q)
+
+    def ship(k):
+        for d in (2, 1, 3):
+            for q in range(NQ):
+                part2[k, d - 1, q * PIECE:(q + 1) * PIECE] = piece(k, q, d).astype(BF16)
         if k:
-            sent((name, "sums out", k - 1), part.at[k - 1])
+            sent(("b", "sums out", k - 1), part2.at[k - 1])
         for d in (2, 1, 3):
-            start((name, "sums out", k), (name, "sums", k), part.at[k, d - 1], x_dev[d],
-                  got.at[k, d - 1])
+            start(("b", "sums out", k), ("b", "sums", k), part2.at[k, d - 1], x_dev[d],
+                  got2.at[k, d - 1])
+        for q in range(NQ):
+            own2[k, q * PIECE:(q + 1) * PIECE] = piece(k, q, 0)
 
     def total(got, kept, name, k):
         arrived((name, "sums", k), got.at[k])
         return kept[k] + (got[k, 0].astype(F32) + got[k, 2].astype(F32)) + got[k, 1].astype(F32)
 
-    for k in range(NCH):
-        own(g1, "a", k)
-    for q in range(NQ):
-        along_x(0, q)
+    own(g1, "a", 0)
+    own(g1, "a", 1)
+    own(g1, "a", 2)
+    along_z(0)
+    along_z(1)
+    along_z(2)
+    along_x(0, 0)
+    along_x(0, 1)
+    along_x(0, 2)
     trace_send(0)
     pair(g1, "a", 0)
-    along_z(0)
     relay(g1, "a", 0, 0)
     pair(g1, "a", 1)
-    along_z(1)
     relay(g1, "a", 1, 0)
-    pair(g1, "a", 2)
-    relay(g1, "a", 2, 0)
     relay_z(0)
     along_x(3, 0)
     along_x(1, 0)
-    trace_sum(0)
-    relay(g1, "a", 0, 1)
+    pair(g1, "a", 2)
+    relay(g1, "a", 2, 0)
     relay_z(1)
     along_x(3, 1)
     along_x(1, 1)
+    trace_sum(0)
+    relay(g1, "a", 0, 1)
+    relay_z(2)
+    along_x(3, 2)
+    along_x(1, 2)
+    for d in (0, 3, 1):
+        to_core(d, 0)
+    relay(g1, "a", 1, 1)
+    to_core(2, 0)
+    relay(g1, "a", 2, 1)
     trace_sum(1)
-    relay(g1, "a", 1, 1)
-    relay(g1, "a", 2, 1)
-    to_core(0)
-    relay_last(0)
-    along_x(2, 0)
-    to_core(3)
-    to_core(1)
     for k in range(NCH):
         far(g1, "a", k, 0)
         far(g1, "a", k, 1)
     for d in (0, 3, 1):
-        from_core(d)
-        if d == 3:
-            relay_last(1)
-            along_x(2, 1)
-        for k in range(NCH):
-            part_dot(g1, k, zs[d], d == 0)
-    to_core(2)
-    from_core(2)
+        from_core(d, 0)
+    from_core(2, 0)
+    for d in (0, 3, 1):
+        to_core(d, 1)
+    early(0)
+    to_core(2, 1)
+    for d in (0, 3, 1):
+        to_core(d, 2)
+    for d in (0, 3, 1):
+        from_core(d, 1)
+    from_core(2, 1)
+    early(1)
+    for d in (0, 3, 1):
+        from_core(d, 2)
     for k in range(NCH):
-        part_dot(g1, k, zs[2])
-        ship(part1, own1, got1, "a", k)
+        for d in (0, 3, 1):
+            part_dot(g1, k, zs[d], d == 0, pl.ds(2 * BAND, BAND))
+    to_core(2, 2)
+    from_core(2, 2)
+    for k in range(NCH):
+        part_dot(g1, k, zs[2], band=pl.ds(2 * BAND, BAND))
+        ship_band(k, 2)
     def squares(k):
         full = total(got1, own1, "a", k)
         for s in range(ROWS // SUB):
@@ -291,7 +337,7 @@
     relay(g2, "b", 2, 0)
     far(g2, "b", 0, 1)
     part_dot(g2, 0, ys[2])
-    ship(part2, own2, got2, "b", 0)
+    ship(0)
     near(g2, "b", 1, 1)
     part_dot(g2, 1, ys[1])
     part_dot(g2, 1, ys[3])
@@ -300,14 +346,14 @@
     far(g2, "b", 1, 1)
     part_dot(g2, 1, ys[2])
     trace_sum(5)
-    ship(part2, own2, got2, "b", 1)
+    ship(1)
     near(g2, "b", 2, 1)
     part_dot(g2, 2, ys[1])
     part_dot(g2, 2, ys[3])
     trace_sum(6)
     far(g2, "b", 2, 1)
     part_dot(g2, 2, ys[2])
-    ship(part2, own2, got2, "b", 2)
+    ship(2)
     trace_sum(7)
 
     trace = jnp.sum(tsend[len(trace_to)], keepdims=True)
@@ -323,31 +369,44 @@
                 up_ref[s * SUB:(s + 1) * SUB, t * BLOCK:(t + 1) * BLOCK] = (
                     lead * a - tail * piece).astype(BF16)
 
-    for g, name, part in ((g1, "a", part1), (g2, "b", part2)):
-        sent((name, "out"), g.at[:, 0:7 * ROWS, :])
-        sent((name, "sums out", NCH - 1), part.at[NCH - 1])
+    sent(("a", "out"), g1.at[:, 0:7 * ROWS, :])
+    sent(("b", "out"), g2.at[:, 0:7 * ROWS, :])
+    sent(("a", "sums out"), part1)
+    sent(("b", "sums out", NCH - 1), part2.at[NCH - 1])
     sent(("z", "out"), zbuf.at[0:3])
     sent(("t", "out"), tsend.at[0:len(trace_to)])
 
     @pl.when(direct)
     def _():
-        sent(("x", "out"), zbuf.at[:, 0])
+        sent(("x", "out"), zbuf.at[0:3, 0])
         sent(("core", "out"), lhs)
 
     @pl.when(jnp.logical_not(direct))
     def _():
-        sent(("x", "out"), zbuf)
+        sent(("x", "out"), zbuf.at[0:3])
+
+
+def publish(sq_ref, up_ref, sq_out, up_out, sems):
+    copies = [pltpu.make_async_copy(sq_ref, sq_out, sems.at[0]),
+              pltpu.make_async_copy(up_ref, up_out, sems.at[1])]
+    for copy in copies:
+        copy.start()
+    for copy in copies:
+        copy.wait()
 
 
 def body(matrix, pattern, shift):
     block = jax.ShapeDtypeStruct((ROWS, COLS), BF16)
     vmem = pl.BlockSpec(memory_space=pltpu.VMEM)
-    return pl.pallas_call(
+    hbm = pl.BlockSpec(memory_space=pltpu.HBM)
+    results = pl.pallas_call(
         kernel,
         out_shape=(block, block),
-        in_specs=[vmem, pl.BlockSpec(memory_space=pltpu.SMEM), vmem],
+        in_specs=[hbm, pl.BlockSpec(memory_space=pltpu.SMEM), hbm],
         out_specs=(vmem, vmem),
         scratch_shapes=[
+            pltpu.VMEM((ROWS, COLS), BF16),
+            pltpu.VMEM((NBLK, BLOCK), F32),
             pltpu.VMEM((NCH, DEPTH, CHUNK), BF16),
             pltpu.VMEM((NCH, DEPTH, CHUNK), BF16),
             pltpu.VMEM((4, 2, ROWS, WIDE), BF16),
@@ -361,14 +420,22 @@
             pltpu.VMEM((NCH, 4 * ROWS, CHUNK), F32),
             pltpu.VMEM((9, 8, BLOCK), F32),
             pltpu.VMEM((8, 8, BLOCK), F32),
-            pltpu.SemaphoreType.DMA((NSEM,)),
+            pltpu.SemaphoreType.DMA((NSEM + 2,)),
         ],
         compiler_params=pltpu.CompilerParams(
-            collective_id=0, has_side_effects=True, vmem_limit_bytes=40 * 2**20),
+            collective_id=0, has_side_effects=True, vmem_limit_bytes=60 * 2**20),
         cost_estimate=pl.CostEstimate(
             flops=4 * ROWS * COLS * ORDER, bytes_accessed=6 * ROWS * COLS, transcendentals=0),
         name="sign_step",
     )(matrix, pattern, shift.reshape(NBLK, BLOCK))
+    return pl.pallas_call(
+        publish,
+        out_shape=(block, block),
+        in_specs=[vmem, vmem],
+        out_specs=(hbm, hbm),
+        scratch_shapes=[pltpu.SemaphoreType.DMA((2,))],
+        name="publish",
+    )(*results)
 
 
 def solution(mesh):

time: 94.6 us -> 88.4 us (0.934)
  local copies, waits for them, and re-layouts: 3.86 us -> 0 us
  Pallas kernels: 88.3 us -> 86.4 us
    unnamed x8 -> x0, local copies, waits for them, and re-layouts: 3.86 us -> none
    pallas_call x1 -> x2, Pallas kernels: 88.3 us -> 86.4 us  [the longest x1 84.6 us: body(): pl.pallas_call(kernel, out_shape=(block, block), in_specs=[hbm, pl.BlockS...]
where the time goes in v3:
time: 88.4 us; the launch traced here: 87.1 us
  Pallas kernels  86.4 us (98%)
    pallas_call x1, Pallas kernels, body(): pl.pallas_call(kernel, out_shape=(block, block), in_specs=[hbm, pl.BlockS...  84.6 us
    pallas_call x1, Pallas kernels, body(): pl.pallas_call(publish, out_shape=(block, block), in_specs=[vmem, vmem],...  1.88 us

profile of v3, /device:TPU:1, one launch (start us, length us, event | category | flops | bytes accessed | tf_op | source)
XLA Modules:
  0.0 87.1 jit_solution(15577265286223356473)
XLA Ops:
  0.6 84.6 %sign_step.1 = (bf16[192,768]{1,0:T(8,128)(2,1)}, bf16[192,768]{1,0:T(8,128)(2,1)}) custom-call(bf16[192,768]{1,0:T(8,128)(2,1)} %m_hbm.1, s32[48,48]{1,0:T(8,128)} %pat_ref.1, f32[48,128]{1,0:T(8,128)} %bitcast.1), custom_call_target="tpu_custom_call" | custom-call | flops 3623878656 | bytes 884736 | tf_op jit(solution)/shard_map/sign_step/pallas_call | solution.py:402
  85.2 1.9 %publish.1 = (bf16[192,768]{1,0:T(8,128)(2,1)}, bf16[192,768]{1,0:T(8,128)(2,1)}) custom-call(bf16[192,768]{1,0:T(8,128)(2,1)} %get-tuple-element.4.sq_ref, bf16[192,768]{1,0:T(8,128)(2,1)} %get-tuple-element.5.up_ref), custom_call_target="tpu_custom_call" | custom-call | tf_op jit(solution)/shard_map/publish/pallas_call | solution.py:431

commit v4 on v3

--- a/solution.py
+++ b/solution.py
@@ -224,20 +224,17 @@
                   got1.at[k, d - 1, band, :])
         own1[k, band] = piece(k, q, 0)
 
-    def early(q):
+    def early(q, k):
         band = pl.ds(q * BAND, BAND)
-        for k in range(NCH):
-            acc[k, band] = jnp.dot(lhs[band, :], g1[k], preferred_element_type=F32)
-            ship_band(k, q)
+        acc[k, band] = jnp.dot(lhs[band, :], g1[k], preferred_element_type=F32)
+        ship_band(k, q)
 
     def ship(k):
         for d in (2, 1, 3):
             for q in range(NQ):
                 part2[k, d - 1, q * PIECE:(q + 1) * PIECE] = piece(k, q, d).astype(BF16)
-        if k:
-            sent(("b", "sums out", k - 1), part2.at[k - 1])
         for d in (2, 1, 3):
-            start(("b", "sums out", k), ("b", "sums", k), part2.at[k, d - 1], x_dev[d],
+            start(("b", "sums out"), ("b", "sums", k), part2.at[k, d - 1], x_dev[d],
                   got2.at[k, d - 1])
         for q in range(NQ):
             own2[k, q * PIECE:(q + 1) * PIECE] = piece(k, q, 0)
@@ -260,41 +257,46 @@
     relay(g1, "a", 0, 0)
     pair(g1, "a", 1)
     relay(g1, "a", 1, 0)
+    pair(g1, "a", 2)
+    relay(g1, "a", 2, 0)
     relay_z(0)
     along_x(3, 0)
     along_x(1, 0)
-    pair(g1, "a", 2)
-    relay(g1, "a", 2, 0)
+    relay(g1, "a", 0, 1)
     relay_z(1)
     along_x(3, 1)
     along_x(1, 1)
-    trace_sum(0)
-    relay(g1, "a", 0, 1)
+    relay(g1, "a", 1, 1)
+    relay(g1, "a", 2, 1)
     relay_z(2)
     along_x(3, 2)
     along_x(1, 2)
     for d in (0, 3, 1):
         to_core(d, 0)
-    relay(g1, "a", 1, 1)
     to_core(2, 0)
-    relay(g1, "a", 2, 1)
-    trace_sum(1)
-    for k in range(NCH):
-        far(g1, "a", k, 0)
-        far(g1, "a", k, 1)
+    far(g1, "a", 0, 0)
+    far(g1, "a", 0, 1)
+    far(g1, "a", 1, 0)
+    far(g1, "a", 1, 1)
+    far(g1, "a", 2, 0)
+    far(g1, "a", 2, 1)
     for d in (0, 3, 1):
         from_core(d, 0)
     from_core(2, 0)
+    for k in range(NCH):
+        early(0, k)
     for d in (0, 3, 1):
         to_core(d, 1)
-    early(0)
     to_core(2, 1)
-    for d in (0, 3, 1):
-        to_core(d, 2)
     for d in (0, 3, 1):
         from_core(d, 1)
     from_core(2, 1)
-    early(1)
+    early(1, 0)
+    early(1, 1)
+    early(1, 2)
+    trace_sum(0)
+    for d in (0, 3, 1):
+        to_core(d, 2)
     for d in (0, 3, 1):
         from_core(d, 2)
     for k in range(NCH):
@@ -305,6 +307,7 @@
     for k in range(NCH):
         part_dot(g1, k, zs[2], band=pl.ds(2 * BAND, BAND))
         ship_band(k, 2)
+    trace_sum(1)
     def squares(k):
         full = total(got1, own1, "a", k)
         for s in range(ROWS // SUB):
@@ -317,24 +320,25 @@
         own(g2, "b", k)
 
     squares(0)
+    squares(1)
     trace_sum(2)
     pair(g2, "b", 0)
     relay(g2, "b", 0, 0)
-    squares(1)
-    trace_sum(3)
-    far_pair(g2, "b", 0)
+    squares(2)
+    part_dot(g2, 0, ys[0], True)
     pair(g2, "b", 1)
     relay(g2, "b", 1, 0)
-    part_dot(g2, 0, ys[0], True)
-    squares(2)
-    trace_sum(4)
+    far_pair(g2, "b", 0)
+    trace_sum(3)
+    part_dot(g2, 1, ys[0], True)
+    pair(g2, "b", 2)
+    relay(g2, "b", 2, 0)
     near(g2, "b", 0, 1)
     part_dot(g2, 0, ys[1])
     part_dot(g2, 0, ys[3])
     far_pair(g2, "b", 1)
-    part_dot(g2, 1, ys[0], True)
-    pair(g2, "b", 2)
-    relay(g2, "b", 2, 0)
+    trace_sum(4)
+    part_dot(g2, 2, ys[0], True)
     far(g2, "b", 0, 1)
     part_dot(g2, 0, ys[2])
     ship(0)
@@ -342,10 +346,9 @@
     part_dot(g2, 1, ys[1])
     part_dot(g2, 1, ys[3])
     far_pair(g2, "b", 2)
-    part_dot(g2, 2, ys[0], True)
+    trace_sum(5)
     far(g2, "b", 1, 1)
     part_dot(g2, 1, ys[2])
-    trace_sum(5)
     ship(1)
     near(g2, "b", 2, 1)
     part_dot(g2, 2, ys[1])
@@ -372,7 +375,7 @@
     sent(("a", "out"), g1.at[:, 0:7 * ROWS, :])
     sent(("b", "out"), g2.at[:, 0:7 * ROWS, :])
     sent(("a", "sums out"), part1)
-    sent(("b", "sums out", NCH - 1), part2.at[NCH - 1])
+    sent(("b", "sums out"), part2)
     sent(("z", "out"), zbuf.at[0:3])
     sent(("t", "out"), tsend.at[0:len(trace_to)])
 

time: 88.4 us -> 85.4 us (0.966)
  Pallas kernels: 86.4 us -> 84.3 us
    pallas_call x1, Pallas kernels: 84.6 us -> 82.4 us  [body(): pl.pallas_call(kernel, out_shape=(block, block), in_specs=[hbm, pl.BlockS...]
where the time goes in v4:
time: 85.4 us; the launch traced here: 85 us
  Pallas kernels  84.3 us (99%)
    pallas_call x1, Pallas kernels, body(): pl.pallas_call(kernel, out_shape=(block, block), in_specs=[hbm, pl.BlockS...  82.4 us
    pallas_call x1, Pallas kernels, body(): pl.pallas_call(publish, out_shape=(block, block), in_specs=[vmem, vmem],...  1.88 us

profile of v4, /device:TPU:1, one launch (start us, length us, event | category | flops | bytes accessed | tf_op | source)
XLA Modules:
  0.0 85.0 jit_solution(5463579043897852106)
XLA Ops:
  0.6 82.4 %sign_step.1 = (bf16[192,768]{1,0:T(8,128)(2,1)}, bf16[192,768]{1,0:T(8,128)(2,1)}) custom-call(bf16[192,768]{1,0:T(8,128)(2,1)} %m_hbm.1, s32[48,48]{1,0:T(8,128)} %pat_ref.1, f32[48,128]{1,0:T(8,128)} %bitcast.1), custom_call_target="tpu_custom_call" | custom-call | flops 3623878656 | bytes 884736 | tf_op jit(solution)/shard_map/sign_step/pallas_call | solution.py:405
  83.1 1.9 %publish.1 = (bf16[192,768]{1,0:T(8,128)(2,1)}, bf16[192,768]{1,0:T(8,128)(2,1)}) custom-call(bf16[192,768]{1,0:T(8,128)(2,1)} %get-tuple-element.4.sq_ref, bf16[192,768]{1,0:T(8,128)(2,1)} %get-tuple-element.5.up_ref), custom_call_target="tpu_custom_call" | custom-call | tf_op jit(solution)/shard_map/publish/pallas_call | solution.py:434

commit v5 on v4

--- a/solution.py
+++ b/solution.py
@@ -62,25 +62,27 @@
     keeps = {}
     ahead = (lax.broadcasted_iota(jnp.int32, (SUB, BLOCK), 0)
              - lax.broadcasted_iota(jnp.int32, (SUB, BLOCK), 1))
-    for s in range(ROWS // SUB):
-        br = lax.div(3 * c + s, 2)
-        for t in range(COLS // BLOCK):
-            bc = 6 * r + t
-            diag = br == bc
-            keep = jnp.where((pat_ref[br, bc] > 0) | diag, 1.0, 0.0).astype(F32)
-            keep_t = jnp.where((pat_ref[bc, br] > 0) | diag, 1.0, 0.0).astype(F32)
-            keeps[s, t] = keep
-            m = m_ref[s * SUB:(s + 1) * SUB, t * BLOCK:(t + 1) * BLOCK].astype(F32)
-            gap = (r * COLS + t * BLOCK) - (c * ROWS + s * SUB)
-            on = jnp.where(ahead == gap, shift_ref[pl.ds(bc, 1), :], 0.0)
-            a = (m * keep + on).astype(BF16)
-            a_t = (m * keep_t + on).astype(BF16)
-            terms += a.astype(F32) * a_t.astype(F32)
-            k, lane = t // 2, (t % 2) * BLOCK
-            g1[k, rows(me, s * SUB, SUB), lane:lane + BLOCK] = a
-            zbuf[zhi, t // 3, s * SUB:(s + 1) * SUB, (t % 3) * BLOCK:(t % 3 + 1) * BLOCK] = a
-    tsend[0] = jnp.sum(terms.reshape(SUB // 8, 8, BLOCK), axis=0)
-
+    def build(part, sums):
+        for s in range(ROWS // SUB):
+            br = lax.div(3 * c + s, 2)
+            for t in (2 * part, 2 * part + 1):
+                bc = 6 * r + t
+                diag = br == bc
+                keep = jnp.where((pat_ref[br, bc] > 0) | diag, 1.0, 0.0).astype(F32)
+                keep_t = jnp.where((pat_ref[bc, br] > 0) | diag, 1.0, 0.0).astype(F32)
+                keeps[s, t] = keep
+                m = m_ref[s * SUB:(s + 1) * SUB, t * BLOCK:(t + 1) * BLOCK].astype(F32)
+                gap = (r * COLS + t * BLOCK) - (c * ROWS + s * SUB)
+                on = jnp.where(ahead == gap, shift_ref[pl.ds(bc, 1), :], 0.0)
+                a = (m * keep + on).astype(BF16)
+                a_t = (m * keep_t + on).astype(BF16)
+                sums += a.astype(F32) * a_t.astype(F32)
+                k, lane = t // 2, (t % 2) * BLOCK
+                g1[k, rows(me, s * SUB, SUB), lane:lane + BLOCK] = a
+                zbuf[zhi, t // 3, s * SUB:(s + 1) * SUB, (t % 3) * BLOCK:(t % 3 + 1) * BLOCK] = a
+        return sums
+
+    terms = build(0, terms)
     pl.semaphore_wait(barrier, len(partners))
 
     index = {}
@@ -244,7 +246,9 @@
         return kept[k] + (got[k, 0].astype(F32) + got[k, 2].astype(F32)) + got[k, 1].astype(F32)
 
     own(g1, "a", 0)
+    terms = build(1, terms)
     own(g1, "a", 1)
+    terms = build(2, terms)
     own(g1, "a", 2)
     along_z(0)
     along_z(1)
@@ -252,6 +256,7 @@
     along_x(0, 0)
     along_x(0, 1)
     along_x(0, 2)
+    tsend[0] = jnp.sum(terms.reshape(SUB // 8, 8, BLOCK), axis=0)
     trace_send(0)
     pair(g1, "a", 0)
     relay(g1, "a", 0, 0)

time: 85.4 us -> 86.3 us (1.011)
  Pallas kernels: 84.3 us -> 85.5 us
    pallas_call x1, Pallas kernels: 82.4 us -> 83.6 us  [body(): pl.pallas_call(kernel, out_shape=(block, block), in_specs=[hbm, pl.BlockS...]
where the time goes in v5:
time: 86.3 us; the launch traced here: 86.1 us
  Pallas kernels  85.5 us (99%)
    pallas_call x1, Pallas kernels, body(): pl.pallas_call(kernel, out_shape=(block, block), in_specs=[hbm, pl.BlockS...  83.6 us
    pallas_call x1, Pallas kernels, body(): pl.pallas_call(publish, out_shape=(block, block), in_specs=[vmem, vmem],...  1.88 us

profile of v5, /device:TPU:1, one launch (start us, length us, event | category | flops | bytes accessed | tf_op | source)
XLA Modules:
  0.0 86.1 jit_solution(8017073460009874403)
XLA Ops:
  0.6 83.6 %sign_step.1 = (bf16[192,768]{1,0:T(8,128)(2,1)}, bf16[192,768]{1,0:T(8,128)(2,1)}) custom-call(bf16[192,768]{1,0:T(8,128)(2,1)} %m_hbm.1, s32[48,48]{1,0:T(8,128)} %pat_ref.1, f32[48,128]{1,0:T(8,128)} %bitcast.1), custom_call_target="tpu_custom_call" | custom-call | flops 3623878656 | bytes 884736 | tf_op jit(solution)/shard_map/sign_step/pallas_call | solution.py:410
  84.2 1.9 %publish.1 = (bf16[192,768]{1,0:T(8,128)(2,1)}, bf16[192,768]{1,0:T(8,128)(2,1)}) custom-call(bf16[192,768]{1,0:T(8,128)(2,1)} %get-tuple-element.4.sq_ref, bf16[192,768]{1,0:T(8,128)(2,1)} %get-tuple-element.5.up_ref), custom_call_target="tpu_custom_call" | custom-call | tf_op jit(solution)/shard_map/publish/pallas_call | solution.py:439
